TPU v7x, 32 devices: a whole 2x2x4 slice. The times are simulated.
32 devices in a mesh: morton: 16 (over z, y, x), chan: 2 (over core).
Axes of the slice: x: 2, y: 2, z: 4, core: 2. Of those that a mesh axis runs over, the one named last changes fastest.
Arguments:
- features: bfloat16 [128, 4, 4, 4, 256], P('morton', None, None, None, 'chan'), may hold values from -6 to 6
- weight: bfloat16 [27, 256, 256], replicated, may hold values from -0.078125 to 0.078125
- neighbours: int32 [128, 27], P('morton'), may hold values from 0 to 24, as said below
- send_slots: int32 [16, 2, 8], P('morton'), may hold values from 0 to 8, as said below
- grad_pooled: bfloat16 [128, 2, 2, 2, 256], P('morton', None, None, None, 'chan'), may hold values from -6 to 6
Outputs:
- pooled: bfloat16 [128, 2, 2, 2, 256], P('morton', None, None, None, 'chan')
- grad_features: bfloat16 [128, 4, 4, 4, 256], P('morton', None, None, None, 'chan')
- grad_weight: float32 [27, 256, 256], P(None, 'chan')
Inputs may be any that keep to these rules, and one draw needn't show every extreme that they name: `neighbours`: entry k = 9 (a + 1) + 3 (e + 1) + (c + 1) of a block names the block at block offset (a, e, c), a along the first octant axis, encoded as in the first step. An offset with a = -1 names a block of the same device or an entry of the previous device's upward list, a = +1 one of the same device or of the next device's downward list, a = 0 one of the same device. The lists come from a grid of blocks: if block b names block c at offset o, block c names b at offset -o. Every occupied slot names itself at offset 13; an empty slot names no block at any offset, and no slot names an empty one or an unused list entry. send_slots[d, 0] lists the slots that device d sends to device d - 1, send_slots[d, 1] those it sends to device d + 1: distinct occupied slots first, then 8 for unused entries. Some device fills both of its lists in every draw. The first device's downward list and the last device's upward list are unused.
All inputs are finite; a program needn't handle non-finite values.
Results may differ from a plain program's by a relative error of at most 0.005.
Values may be sent and summed in bfloat16 or wider, within the bound.
A program may use at most 128 MiB of HBM per device.

v0:
```python
import functools

import jax
import jax.numpy as jnp
from jax import lax
from jax.experimental import pallas as pl
from jax.experimental.pallas import tpu as pltpu
from jax.sharding import PartitionSpec as P

MESH = pl.DeviceIdType.MESH
F32 = jnp.float32
BF16 = jnp.bfloat16


def offsets_of(x):
    return ([-1] if x == 3 else []) + [0] + ([1] if x == 0 else [])


def place(offset, x):
    return 0 if offset < 0 else (5 if offset > 0 else x + 1)


def rim_copies(own, low, high, send, recv, me, core, n):
    nxt, prv = lax.rem(me + 1, n), lax.rem(me + n - 1, n)
    rows = own.shape[1]
    plane = rows // 4
    peer = 1 - core
    copies = [
        pltpu.make_async_remote_copy(
            src_ref=own.at[core], dst_ref=own.at[core], send_sem=send.at[0],
            recv_sem=recv.at[0], device_id=(me, peer), device_id_type=MESH,
        )
    ]
    for target in range(2):
        copies.append(
            pltpu.make_async_remote_copy(
                src_ref=own.at[core, pl.ds(rows - plane, plane)], dst_ref=low.at[core],
                send_sem=send.at[1 + target], recv_sem=recv.at[1 + core],
                device_id=(nxt, target), device_id_type=MESH,
            )
        )
        copies.append(
            pltpu.make_async_remote_copy(
                src_ref=own.at[core, pl.ds(0, plane)], dst_ref=high.at[core],
                send_sem=send.at[3 + target], recv_sem=recv.at[3 + core],
                device_id=(prv, target), device_id_type=MESH,
            )
        )
    return copies


def wait_peer(own, send, recv, me, core):
    pltpu.make_async_remote_copy(
        src_ref=own.at[1 - core], dst_ref=own.at[1 - core], send_sem=send.at[0],
        recv_sem=recv.at[0], device_id=(me, 1 - core), device_id_type=MESH,
    ).wait_recv()


def wait_rims(own, low, high, send, recv, me, core):
    for half in range(2):
        for ref, base in ((low, 1), (high, 3)):
            pltpu.make_async_remote_copy(
                src_ref=ref.at[half], dst_ref=ref.at[half], send_sem=send.at[0],
                recv_sem=recv.at[base + half], device_id=(me, 1 - core), device_id_type=MESH,
            ).wait_recv()


def fill_interior(tile, own, occ, half, blocks):
    value = own[half].astype(F32).reshape(4, 4, 4, blocks, own.shape[-1])
    tile[half, 1:5, 1:5, 1:5] = value * occ


def fill_border(tile, low, high, pick, blocks):
    width = low.shape[-1]
    for x in range(4):
        for y in range(4):
            for z in range(4):
                ks = [
                    (a, e, c)
                    for a in offsets_of(x)
                    for e in offsets_of(y)
                    for c in offsets_of(z)
                    if (a, e, c) != (0, 0, 0)
                ]
                if not ks:
                    continue
                left = jnp.concatenate(
                    [pick[9 * a + 3 * e + c + 13] for a, e, c in ks], axis=0
                )
                own = jnp.concatenate([tile[h, 1 + x, 1 + y, 1 + z] for h in range(2)], axis=1)
                if x in (0, 3):
                    rim = high if x == 0 else low
                    r = (4 * y + z) * blocks
                    other = jnp.concatenate(
                        [rim[h, r : r + blocks, :].astype(F32) for h in range(2)], axis=1
                    )
                    right = jnp.concatenate([own, other], axis=0)
                else:
                    right = own
                got = jnp.dot(
                    left[:, : right.shape[0]].astype(BF16), right.astype(BF16),
                    preferred_element_type=F32,
                )
                for j, (a, e, c) in enumerate(ks):
                    for h in range(2):
                        tile[h, place(a, x), place(e, y), place(c, z)] = got[
                            j * blocks : (j + 1) * blocks, h * width : (h + 1) * width
                        ]


def window(tile, half, a, e, c):
    part = tile[half, a : a + 4, e : e + 4, c : c + 4]
    return part.reshape(-1, part.shape[-1]).astype(BF16)


def kernel(
    n, feat_ref, weight_ref, names_ref, occ_ref, sel_ref, gp_ref,
    pooled_ref, gf_ref, gw_ref,
    wf, wb, feat, flow, fhigh, grad, glow, ghigh, tile_in, tile_g, pick, merge,
    stage, pool_stage, wsem, fsend, frecv, gsend, grecv, ssend, srecv,
):
    me, core = lax.axis_index("morton"), lax.axis_index("chan")
    nxt, prv = lax.rem(me + 1, n), lax.rem(me + n - 1, n)
    width = feat_ref.shape[-1]
    rows = feat_ref.shape[0]
    blocks = rows // 64
    columns = pl.ds(pl.multiple_of(core * width, width), width)
    load_f = pltpu.make_async_copy(weight_ref.at[:, :, columns], wf, wsem.at[0])
    load_b = pltpu.make_async_copy(weight_ref.at[:, columns, :], wb, wsem.at[1])
    load_f.start()
    load_b.start()
    barrier = pltpu.get_barrier_semaphore()
    for target in ((me, 1 - core), (nxt, 0), (nxt, 1), (prv, 0), (prv, 1)):
        pl.semaphore_signal(barrier, inc=1, device_id=target, device_id_type=MESH)
    stage[...] = feat_ref[...].astype(F32)
    feat[core] = jnp.concatenate(
        [stage[pl.ds(p, blocks, stride=64), :] for p in range(64)], axis=0
    ).astype(BF16)
    pl.semaphore_wait(barrier, 5)
    sels = [
        pltpu.make_async_remote_copy(
            src_ref=sel_ref.at[1], dst_ref=merge.at[0], send_sem=ssend.at[0],
            recv_sem=srecv.at[0], device_id=(nxt, core), device_id_type=MESH,
        ),
        pltpu.make_async_remote_copy(
            src_ref=sel_ref.at[0], dst_ref=merge.at[1], send_sem=ssend.at[1],
            recv_sem=srecv.at[1], device_id=(prv, core), device_id_type=MESH,
        ),
    ]
    copies = rim_copies(feat, flow, fhigh, fsend, frecv, me, core, n)
    for copy in sels + copies:
        copy.start()
    occ = occ_ref[...]
    fill_interior(tile_in, feat, occ, core, blocks)
    for copy in sels:
        copy.wait()
    eye = (
        lax.broadcasted_iota(jnp.int32, (blocks, width), 0)
        == lax.broadcasted_iota(jnp.int32, (blocks, width), 1)
    ).astype(F32)
    pick[0:9] = jnp.dot(
        names_ref[0:9].reshape(9 * blocks, width)[:, : 2 * blocks],
        jnp.concatenate([eye, merge[0]], axis=0), preferred_element_type=F32,
    ).reshape(9, blocks, width)
    pick[9:18] = names_ref[9:18]
    pick[18:27] = jnp.dot(
        names_ref[18:27].reshape(9 * blocks, width)[:, : 2 * blocks],
        jnp.concatenate([eye, merge[1]], axis=0), preferred_element_type=F32,
    ).reshape(9, blocks, width)
    wait_peer(feat, fsend, frecv, me, core)
    fill_interior(tile_in, feat, occ, 1 - core, blocks)
    wait_rims(feat, flow, fhigh, fsend, frecv, me, core)
    fill_border(tile_in, flow, fhigh, pick, blocks)
    load_f.wait()
    acc = None
    for a in range(3):
        for e in range(3):
            left = jnp.concatenate(
                [window(tile_in, h, a, e, c) for c in range(3) for h in range(2)], axis=1
            )
            k = 9 * a + 3 * e
            right = wf[k : k + 3].reshape(6 * width, width)
            term = jnp.dot(left, right, preferred_element_type=F32)
            acc = term if acc is None else acc + term
    s = jax.nn.sigmoid(acc)
    act = (acc * s).reshape(2, 2, 2, 2, 2, 2, blocks, width)
    summed = act[:, 0] + act[:, 1]
    summed = summed[:, :, 0] + summed[:, :, 1]
    summed = summed[:, :, :, 0] + summed[:, :, :, 1]
    slope = (s * (1.0 + acc * (1.0 - s))).reshape(2, 2, 2, 2, 2, 2, blocks, width)
    pool_stage[0] = gp_ref[...].astype(F32) * 0.125
    for x in range(2):
        for y in range(2):
            for z in range(2):
                q = 4 * x + 2 * y + z
                g = pool_stage[0, pl.ds(q, blocks, stride=8), :]
                pool_stage[1, pl.ds(q, blocks, stride=8), :] = summed[x, y, z] * 0.125
                for i in range(2):
                    for j in range(2):
                        for l in range(2):
                            p = 16 * (2 * x + i) + 4 * (2 * y + j) + 2 * z + l
                            stage[p * blocks : (p + 1) * blocks, :] = g * slope[x, i, y, j, z, l]
    grad[core] = stage[...].astype(BF16)
    pooled_ref[...] = pool_stage[1].astype(BF16)
    gcopies = rim_copies(grad, glow, ghigh, gsend, grecv, me, core, n)
    for copy in gcopies:
        copy.start()
    fill_interior(tile_g, grad, occ, core, blocks)
    wait_peer(grad, gsend, grecv, me, core)
    fill_interior(tile_g, grad, occ, 1 - core, blocks)
    flipped = jnp.concatenate([grad[0], grad[1]], axis=1).T
    for k in range(27):
        gw_ref[k] = jnp.dot(
            flipped, window(tile_in, core, k // 9, k // 3 % 3, k % 3), preferred_element_type=F32
        )
    wait_rims(grad, glow, ghigh, gsend, grecv, me, core)
    fill_border(tile_g, glow, ghigh, pick, blocks)
    load_b.wait()
    acc = None
    for a in range(3):
        for e in range(3):
            left = jnp.concatenate(
                [window(tile_g, h, 2 - a, 2 - e, 2 - c) for c in range(3) for h in range(2)],
                axis=1,
            )
            k = 9 * a + 3 * e
            right = jnp.concatenate([wb[k + c] for c in range(3)], axis=1)
            term = lax.dot_general(
                left, right, (((1,), (1,)), ((), ())), preferred_element_type=F32
            )
            acc = term if acc is None else acc + term
    for p in range(64):
        stage[pl.ds(p, blocks, stride=64), :] = acc[p * blocks : (p + 1) * blocks]
    gf_ref[...] = stage[...].astype(BF16)
    for copy in copies + gcopies:
        copy.wait_send()


def body(features, weight, neighbours, send_slots, grad_pooled):
    n = lax.axis_size("morton")
    blocks = features.shape[0]
    width = features.shape[-1]
    full = weight.shape[-1]
    slots = send_slots.shape[-1]
    lanes = jnp.arange(width, dtype=jnp.int32)
    column = jnp.where(neighbours > blocks, neighbours - 1, neighbours)
    column = jnp.where(neighbours > blocks + slots, column - slots, column)
    column = jnp.where(neighbours == blocks, -1, column)
    names = (column.T[:, :, None] == lanes).astype(F32)
    occ = jnp.broadcast_to((neighbours[:, 13] < blocks).astype(F32)[:, None], (blocks, width))
    places = jnp.where(send_slots[0] < blocks, send_slots[0] + blocks, -1)
    sel = (places[:, :, None] == lanes).astype(F32)
    rows = blocks * 64
    vmem = pl.BlockSpec(memory_space=pltpu.VMEM)
    pooled, gf, gw = pl.pallas_call(
        functools.partial(kernel, n),
        out_shape=(
            jax.ShapeDtypeStruct((blocks * 8, width), BF16),
            jax.ShapeDtypeStruct((rows, width), BF16),
            jax.ShapeDtypeStruct((27, full, width), F32),
        ),
        in_specs=[vmem, pl.BlockSpec(memory_space=pl.ANY), vmem, vmem, vmem, vmem],
        out_specs=(vmem, vmem, vmem),
        scratch_shapes=[
            pltpu.VMEM((27, full, width), BF16),
            pltpu.VMEM((27, width, full), BF16),
            pltpu.VMEM((2, rows, width), BF16),
            pltpu.VMEM((2, rows // 4, width), BF16),
            pltpu.VMEM((2, rows // 4, width), BF16),
            pltpu.VMEM((2, rows, width), BF16),
            pltpu.VMEM((2, rows // 4, width), BF16),
            pltpu.VMEM((2, rows // 4, width), BF16),
            pltpu.VMEM((2, 6, 6, 6, blocks, width), F32),
            pltpu.VMEM((2, 6, 6, 6, blocks, width), F32),
            pltpu.VMEM((27, blocks, width), F32),
            pltpu.VMEM((2, slots, width), F32),
            pltpu.VMEM((rows, width), F32),
            pltpu.VMEM((2, blocks * 8, width), F32),
            pltpu.SemaphoreType.DMA((2,)),
            pltpu.SemaphoreType.DMA((5,)),
            pltpu.SemaphoreType.DMA((5,)),
            pltpu.SemaphoreType.DMA((5,)),
            pltpu.SemaphoreType.DMA((5,)),
            pltpu.SemaphoreType.DMA((2,)),
            pltpu.SemaphoreType.DMA((2,)),
        ],
        compiler_params=pltpu.CompilerParams(
            collective_id=0, has_side_effects=True, vmem_limit_bytes=48 * 1024 * 1024
        ),
    )(
        features.reshape(rows, width), weight, names, occ, sel,
        grad_pooled.reshape(blocks * 8, width),
    )
    gw = lax.psum(gw, "morton")
    return (
        pooled.reshape(grad_pooled.shape),
        gf.reshape(features.shape),
        jnp.swapaxes(gw, 1, 2),
    )


def solution(mesh):
    in_specs = (
        P("morton", None, None, None, "chan"),
        P(),
        P("morton", None),
        P("morton", None, None),
        P("morton", None, None, None, "chan"),
    )
    out_specs = (
        P("morton", None, None, None, "chan"),
        P("morton", None, None, None, "chan"),
        P(None, "chan", None),
    )
    return jax.shard_map(body, mesh=mesh, in_specs=in_specs, out_specs=out_specs, check_vma=False)
```

profile of v0, /device:TPU:0, one launch (start us, length us, event | category | flops | bytes accessed | tf_op | source)
XLA Modules:
  0.0 203.6 jit_solution(11147295916273433306)
XLA Ops:
  7.2 0.0 all-reduce.2.cloned.1.call-start
  7.2 0.9 convert_reduce_fusion
  8.1 0.7 fusion.3
  8.8 0.7 fusion.4
  9.5 0.1 fusion.1.sel_ref
  9.5 0.1 copy.8
  9.6 0.1 fusion.names_ref
  9.7 0.1 broadcast_in_dim.26.occ_ref
  9.8 0.0 copy-start
  9.8 0.9 copy-done
  10.7 0.0 copy-start.1
  10.7 0.7 copy-done.1
  11.4 25.4 %shard_map.76 = (bf16[64,128]{1,0:T(8,128)(2,1)S(1)}, bf16[512,128]{1,0:T(8,128)(2,1)S(1)}, f32[27,256,128]{2,1,0:T(8,128)}) custom-call(bf16[512,128]{1,0:T(8,128)(2,1)S(1)} %bitcast.10, bf16[27,256,256]{2,1,0:T(8,128)(2,1)} %weight_ref.1, f32[27,8,128]{2,1,0:T(8,128)S(1)} %fusion.names_ref, f32[8,128]{1,0:T(8,128)S(1)} %broadcast_in_dim.26.occ_ref, ...), custom_call_target="tpu_custom_call" | custom-call | tf_op jit(solution)/shard_map/pallas_call | solution.py:255
  36.9 0.0 all-reduce.2.cloned.1.call-update
  36.9 153.4 %all-reduce.2.cloned.1.call-done = f32[27,128,256]{1,2,0:T(8,128)} async-done(((f32[27,128,256]{1,2,0:T(8,128)}), f32[27,128,256]{1,2,0:T(8,128)}) %all-reduce.2.cloned.1.call-update) | async-done | bytes 3538960 | tf_op jit(solution)/shard_map/psum | solution.py:294
  190.3 5.2 %copy.9 = f32[27,128,256]{2,1,0:T(8,128)} copy(f32[27,128,256]{1,2,0:T(8,128)} %all-reduce.2.cloned.1.call-done) | data formatting | bytes 7077888
  195.5 0.6 copy.13
  196.1 0.7 copy.14
Async XLA Ops:
  7.2 183.2 %all-reduce.2.cloned.1.call-start = ((), (), s32[]{:S(2)}) async-start(), calls=%async_computation | async-start | bytes 7077888 | tf_op jit(solution)/shard_map/psum | solution.py:294
  9.8 0.9 copy-start
  10.7 0.7 copy-start.1
Sparse Core Ops, SparseCore 0:
  37.0 153.2 all-reduce.1
where the time goes:
time: 204 us
  waiting for transfers between devices  153 us (75%)
  Pallas kernels  25.4 us (12%)
  between operations  14 us (7%)
  local copies, waits for them, and re-layouts  8.19 us (4%)
  other arithmetic  2.41 us (1%)
    psum x1, waiting for transfers between devices, body(): gw = lax.psum(gw, 'morton')  153 us
    pallas_call x1, Pallas kernels, body(): pl.pallas_call(functools.partial(kernel, n), out_shape=(jax.ShapeDtypeStr...  25.4 us
    unnamed x7, local copies, waits for them, and re-layouts  8.03 us
  transfers between devices with their start and end apart: 1, of which 1 were waited for; matrix products, arithmetic and copies ran while one was open for 0% of the time, Pallas kernels for 0%

commit v1 on v0

--- a/solution.py
+++ b/solution.py
@@ -113,11 +113,91 @@
     return part.reshape(-1, part.shape[-1]).astype(BF16)
 
 
+CUTS = (0, 7, 14, 21, 27)
+
+
+def bit_orders(n):
+    bits = []
+    while 2 ** len(bits) < n:
+        bits.append(2 ** len(bits))
+    swapped = bits[1::-1] + bits[2:]
+    return (bits, swapped)
+
+
+class Summing:
+    def __init__(self, piece, n, me, core, acc, out, sends, recvs, sem):
+        self.k0, self.k1 = CUTS[piece], CUTS[piece + 1]
+        self.piece, self.me, self.core = piece, me, core
+        self.acc, self.out, self.sends, self.recvs = acc, out, sends, recvs
+        self.sem = sem
+        self.bits = bit_orders(n)[piece % 2]
+        self.low, self.size = 0, acc.shape[1]
+        self.trail, self.pending = [], None
+
+    def partner(self, bit):
+        mine = lax.rem(lax.div(self.me, bit), 2)
+        return mine, self.me + bit * (1 - 2 * mine)
+
+    def rows(self, low, size):
+        if isinstance(low, int):
+            return pl.ds(low, size)
+        return pl.ds(pl.multiple_of(low, 16), size)
+
+    def copy(self, step, src, dst, to):
+        pair = self.sem.at[self.piece, step]
+        return pltpu.make_async_remote_copy(
+            src_ref=src, dst_ref=dst, send_sem=pair.at[0], recv_sem=pair.at[1],
+            device_id=(to, self.core), device_id_type=MESH,
+        )
+
+    def start_sum(self, step):
+        ks = pl.ds(self.k0, self.k1 - self.k0)
+        mine, to = self.partner(self.bits[step])
+        halves = self.size > 16
+        part = self.size // 2 if halves else self.size
+        gone = self.low + (1 - mine) * part if halves else self.low
+        kept = self.low + mine * part if halves else self.low
+        send = self.sends[step].at[ks]
+        send[...] = self.acc[ks, self.rows(gone, part), :].astype(BF16)
+        copy = self.copy(step, send, self.recvs[step].at[ks], to)
+        copy.start()
+        self.pending = copy
+        self.trail.append((self.bits[step], halves, self.low, self.size))
+        self.low, self.size = kept, part
+
+    def end_sum(self, step):
+        ks = pl.ds(self.k0, self.k1 - self.k0)
+        self.pending.wait()
+        rows = self.rows(self.low, self.size)
+        own = self.acc[ks, rows, :]
+        if not self.trail[-1][1]:
+            own = self.sends[step][ks].astype(F32)
+        total = own + self.recvs[step][ks].astype(F32)
+        if step + 1 < len(self.bits):
+            self.acc[ks, rows, :] = total
+        else:
+            self.out[ks, rows, :] = total.astype(BF16)
+            self.trail = [t for t in self.trail if t[1]]
+
+    def start_gather(self, step):
+        bit, _, low, size = self.trail[-1 - step]
+        ks = pl.ds(self.k0, self.k1 - self.k0)
+        _, to = self.partner(bit)
+        held = self.out.at[ks, self.rows(self.low, self.size)]
+        copy = self.copy(len(self.bits) + step, held, held, to)
+        copy.start()
+        self.pending = copy
+        self.low, self.size = low, size
+
+    def end_gather(self):
+        self.pending.wait()
+
+
 def kernel(
     n, feat_ref, weight_ref, names_ref, occ_ref, sel_ref, gp_ref,
     pooled_ref, gf_ref, gw_ref,
     wf, wb, feat, flow, fhigh, grad, glow, ghigh, tile_in, tile_g, pick, merge,
-    stage, pool_stage, wsem, fsend, frecv, gsend, grecv, ssend, srecv,
+    stage, pool_stage, wsem, fsend, frecv, gsend, grecv, ssend, srecv, total, rsem, *bufs,
 ):
     me, core = lax.axis_index("morton"), lax.axis_index("chan")
     nxt, prv = lax.rem(me + 1, n), lax.rem(me + n - 1, n)
@@ -130,13 +210,19 @@
     load_f.start()
     load_b.start()
     barrier = pltpu.get_barrier_semaphore()
-    for target in ((me, 1 - core), (nxt, 0), (nxt, 1), (prv, 0), (prv, 1)):
+    steps = len(bufs) // 2
+    sums = [
+        Summing(i, n, me, core, total, gw_ref, bufs[:steps], bufs[steps:], rsem)
+        for i in range(len(CUTS) - 1)
+    ]
+    others = [(sums[0].partner(bit)[1], core) for bit in sums[0].bits]
+    for target in [(me, 1 - core), (nxt, 0), (nxt, 1), (prv, 0), (prv, 1)] + others:
         pl.semaphore_signal(barrier, inc=1, device_id=target, device_id_type=MESH)
     stage[...] = feat_ref[...].astype(F32)
     feat[core] = jnp.concatenate(
         [stage[pl.ds(p, blocks, stride=64), :] for p in range(64)], axis=0
     ).astype(BF16)
-    pl.semaphore_wait(barrier, 5)
+    pl.semaphore_wait(barrier, 5 + len(others))
     sels = [
         pltpu.make_async_remote_copy(
             src_ref=sel_ref.at[1], dst_ref=merge.at[0], send_sem=ssend.at[0],
@@ -209,10 +295,13 @@
     wait_peer(grad, gsend, grecv, me, core)
     fill_interior(tile_g, grad, occ, 1 - core, blocks)
     flipped = jnp.concatenate([grad[0], grad[1]], axis=1).T
-    for k in range(27):
-        gw_ref[k] = jnp.dot(
-            flipped, window(tile_in, core, k // 9, k // 3 % 3, k % 3), preferred_element_type=F32
-        )
+    for one in sums:
+        for k in range(one.k0, one.k1):
+            total[k] = jnp.dot(
+                flipped, window(tile_in, core, k // 9, k // 3 % 3, k % 3),
+                preferred_element_type=F32,
+            )
+        one.start_sum(0)
     wait_rims(grad, glow, ghigh, gsend, grecv, me, core)
     fill_border(tile_g, glow, ghigh, pick, blocks)
     load_b.wait()
@@ -232,6 +321,19 @@
     for p in range(64):
         stage[pl.ds(p, blocks, stride=64), :] = acc[p * blocks : (p + 1) * blocks]
     gf_ref[...] = stage[...].astype(BF16)
+    for step in range(steps):
+        for one in sums:
+            one.end_sum(step)
+            if step + 1 < steps:
+                one.start_sum(step + 1)
+            else:
+                one.start_gather(0)
+    gathers = len(sums[0].trail)
+    for step in range(1, gathers + 1):
+        for one in sums:
+            one.end_gather()
+            if step < gathers:
+                one.start_gather(step)
     for copy in copies + gcopies:
         copy.wait_send()
 
@@ -251,13 +353,16 @@
     places = jnp.where(send_slots[0] < blocks, send_slots[0] + blocks, -1)
     sel = (places[:, :, None] == lanes).astype(F32)
     rows = blocks * 64
+    steps = len(bit_orders(n)[0])
+    sizes = [max(full >> (step + 1), 16) for step in range(steps)]
+    buffers = [pltpu.VMEM((27, size, width), BF16) for size in sizes]
     vmem = pl.BlockSpec(memory_space=pltpu.VMEM)
     pooled, gf, gw = pl.pallas_call(
         functools.partial(kernel, n),
         out_shape=(
             jax.ShapeDtypeStruct((blocks * 8, width), BF16),
             jax.ShapeDtypeStruct((rows, width), BF16),
-            jax.ShapeDtypeStruct((27, full, width), F32),
+            jax.ShapeDtypeStruct((27, full, width), BF16),
         ),
         in_specs=[vmem, pl.BlockSpec(memory_space=pl.ANY), vmem, vmem, vmem, vmem],
         out_specs=(vmem, vmem, vmem),
@@ -283,7 +388,10 @@
             pltpu.SemaphoreType.DMA((5,)),
             pltpu.SemaphoreType.DMA((2,)),
             pltpu.SemaphoreType.DMA((2,)),
-        ],
+            pltpu.VMEM((27, full, width), F32),
+            pltpu.SemaphoreType.DMA((len(CUTS) - 1, 2 * steps, 2)),
+        ]
+        + buffers * 2,
         compiler_params=pltpu.CompilerParams(
             collective_id=0, has_side_effects=True, vmem_limit_bytes=48 * 1024 * 1024
         ),
@@ -291,11 +399,10 @@
         features.reshape(rows, width), weight, names, occ, sel,
         grad_pooled.reshape(blocks * 8, width),
     )
-    gw = lax.psum(gw, "morton")
     return (
         pooled.reshape(grad_pooled.shape),
         gf.reshape(features.shape),
-        jnp.swapaxes(gw, 1, 2),
+        jnp.swapaxes(gw, 1, 2).astype(F32),
     )
 
 

time: 204 us -> 82 us (0.40)
  waiting for transfers between devices: 153 us -> 0 us
  Pallas kernels: 25.4 us -> 66.2 us
  between operations: 14 us -> 0.66 us
  other arithmetic: 2.41 us -> 4.57 us
    psum x1 -> x0, waiting for transfers between devices: 153 us -> none  [body(): gw = lax.psum(gw, 'morton')]
    pallas_call x1, Pallas kernels: 25.4 us -> 66.2 us  [body(): pl.pallas_call(functools.partial(kernel, n), out_shape=(jax.ShapeDtypeStr...]
    convert_element_type x0 -> x1, other arithmetic: none -> 2.16 us  [body(): jnp.swapaxes(gw, 1, 2).astype(F32)]
    unnamed x7 -> x9, local copies, waits for them, and re-layouts: 8.03 us -> 10 us
  transfers between devices with their start and end apart: 1 -> 0, of which waited for: 1 -> 0; matrix products, arithmetic and copies ran while one was open for 0% -> 0% of each run, Pallas kernels for 0% -> 0%
where the time goes in v1:
time: 82 us; the launch traced here: 81.6 us
  Pallas kernels  66.2 us (81%)
  local copies, waits for them, and re-layouts  10.2 us (12%)
  other arithmetic  4.57 us (6%)
    pallas_call x1, Pallas kernels, body(): pl.pallas_call(functools.partial(kernel, n), out_shape=(jax.ShapeDtypeStr...  66.2 us
    unnamed x9, local copies, waits for them, and re-layouts  10 us
    convert_element_type x1, other arithmetic, body(): jnp.swapaxes(gw, 1, 2).astype(F32)  2.16 us

profile of v1, /device:TPU:0, one launch (start us, length us, event | category | flops | bytes accessed | tf_op | source)
XLA Modules:
  0.0 81.6 jit_solution(12733353098849067599)
XLA Ops:
  0.6 0.9 %convert_reduce_fusion = f32[8]{0:T(128)S(1)} fusion(s32[8,27]{1,0:T(8,128)} %param.7), kind=kLoop, calls=%fused_computation.9 | loop fusion | flops 16 | bytes 64 | tf_op jit(solution)/shard_map/broadcast_in_dim | solution.py:352
  1.5 0.7 fusion.4
  2.2 0.1 broadcast_in_dim.26.occ_ref
  2.3 0.7 fusion.3
  2.9 0.1 fusion.1.sel_ref
  3.0 0.1 copy.8
  3.1 0.1 fusion.names_ref
  3.2 0.0 copy-start
  3.2 2.0 %copy-done = bf16[27,256,256]{2,1,0:T(8,128)(2,1)S(1)} copy-done((bf16[27,256,256]{2,1,0:T(8,128)(2,1)S(1)}, bf16[27,256,256]{2,1,0:T(8,128)(2,1)}, u32[]{:S(2)}) %copy-start) | copy-done | bytes 3538968
  5.2 0.0 copy-start.1
  5.2 0.9 %copy-done.1 = bf16[8,4,4,4,128]{4,3,2,1,0:T(4,128)(2,1)S(1)} copy-done((bf16[8,4,4,4,128]{4,3,2,1,0:T(4,128)(2,1)S(1)}, bf16[8,4,4,4,128]{4,3,2,1,0:T(4,128)(2,1)}, u32[]{:S(2)}) %copy-start.1) | copy-done | bytes 131096
  6.1 0.0 copy-start.2
  6.1 0.7 copy-done.2
  6.8 66.2 %shard_map.76 = (bf16[64,128]{1,0:T(8,128)(2,1)S(1)}, bf16[512,128]{1,0:T(8,128)(2,1)S(1)}, bf16[27,256,128]{2,1,0:T(8,128)(2,1)S(1)}) custom-call(bf16[512,128]{1,0:T(8,128)(2,1)S(1)} %bitcast.11, bf16[27,256,256]{2,1,0:T(8,128)(2,1)S(1)} %copy-done, f32[27,8,128]{2,1,0:T(8,128)S(1)} %fusion.names_ref, f32[8,128]{1,0:T(8,128)S(1)} %broadcast_in_dim.26.occ_ref, ...), custom_call_target="tpu_custom_call" | custom-call | tf_op jit(solution)/shard_map/pallas_call | solution.py:360
  73.0 2.2 %convert_bitcast_fusion = f32[27,128,256]{1,2,0:T(8,128)} fusion(bf16[27,256,128]{2,1,0:T(8,128)(2,1)S(1)} %get-tuple-element.8), kind=kLoop, calls=%fused_computation | loop fusion | flops 884736 | bytes 5308416 | tf_op jit(solution)/shard_map/convert_element_type | solution.py:405
  75.2 5.2 %copy.9 = f32[27,128,256]{2,1,0:T(8,128)} copy(f32[27,128,256]{1,2,0:T(8,128)} %convert_bitcast_fusion) | data formatting | bytes 7077888
  80.3 0.6 copy.12
  80.9 0.7 copy.13
Async XLA Ops:
  3.2 2.0 %copy-start = (bf16[27,256,256]{2,1,0:T(8,128)(2,1)S(1)}, bf16[27,256,256]{2,1,0:T(8,128)(2,1)}, u32[]{:S(2)}) copy-start(bf16[27,256,256]{2,1,0:T(8,128)(2,1)} %weight_ref.1) | copy-start | bytes 10616836
  5.2 0.9 %copy-start.1 = (bf16[8,4,4,4,128]{4,3,2,1,0:T(4,128)(2,1)S(1)}, bf16[8,4,4,4,128]{4,3,2,1,0:T(4,128)(2,1)}, u32[]{:S(2)}) copy-start(bf16[8,4,4,4,128]{4,3,2,1,0:T(4,128)(2,1)} %param.5) | copy-start | bytes 393220
  6.1 0.7 copy-start.2

commit v2 on v1

--- a/solution.py
+++ b/solution.py
@@ -113,15 +113,17 @@
     return part.reshape(-1, part.shape[-1]).astype(BF16)
 
 
-CUTS = (0, 7, 14, 21, 27)
+CUTS = (0, 5, 10, 14, 19, 24, 27)
 
 
 def bit_orders(n):
     bits = []
     while 2 ** len(bits) < n:
         bits.append(2 ** len(bits))
-    swapped = bits[1::-1] + bits[2:]
-    return (bits, swapped)
+    if len(bits) < 4:
+        return (bits, bits[::-1], bits)
+    x, y, near, far = bits[:4]
+    return (bits, [y, near, far, x] + bits[4:], [near, x, y, far] + bits[4:])
 
 
 class Summing:
@@ -130,7 +132,7 @@
         self.piece, self.me, self.core = piece, me, core
         self.acc, self.out, self.sends, self.recvs = acc, out, sends, recvs
         self.sem = sem
-        self.bits = bit_orders(n)[piece % 2]
+        self.bits = bit_orders(n)[piece % 3]
         self.low, self.size = 0, acc.shape[1]
         self.trail, self.pending = [], None
 
@@ -297,10 +299,13 @@
     flipped = jnp.concatenate([grad[0], grad[1]], axis=1).T
     for one in sums:
         for k in range(one.k0, one.k1):
-            total[k] = jnp.dot(
+            term = jnp.dot(
                 flipped, window(tile_in, core, k // 9, k // 3 % 3, k % 3),
                 preferred_element_type=F32,
             )
+            for half in range(2):
+                span = slice(half * width, (half + 1) * width)
+                total[k, span] = term[span].T
         one.start_sum(0)
     wait_rims(grad, glow, ghigh, gsend, grecv, me, core)
     fill_border(tile_g, glow, ghigh, pick, blocks)
@@ -393,7 +398,7 @@
         ]
         + buffers * 2,
         compiler_params=pltpu.CompilerParams(
-            collective_id=0, has_side_effects=True, vmem_limit_bytes=48 * 1024 * 1024
+            collective_id=0, has_side_effects=True, vmem_limit_bytes=60 * 1024 * 1024
         ),
     )(
         features.reshape(rows, width), weight, names, occ, sel,
@@ -402,7 +407,7 @@
     return (
         pooled.reshape(grad_pooled.shape),
         gf.reshape(features.shape),
-        jnp.swapaxes(gw, 1, 2).astype(F32),
+        jnp.swapaxes(gw.reshape(27, 2, width, width), 1, 2).reshape(27, width, full).astype(F32),
     )
 
 

time: 82 us -> 68.2 us (0.83)
  Pallas kernels: 66.2 us -> 57.9 us
  local copies, waits for them, and re-layouts: 10.2 us -> 2.02 us
  other arithmetic: 4.57 us -> 7.38 us
    unnamed x9 -> x6, local copies, waits for them, and re-layouts: 10 us -> 1.27 us
    pallas_call x1, Pallas kernels: 66.2 us -> 57.9 us  [body(): pl.pallas_call(functools.partial(kernel, n), out_shape=(jax.ShapeDtypeStr...]
    convert_element_type x1, other arithmetic: 2.16 us -> 3.72 us  [body(): jnp.swapaxes(gw.reshape(27, 2, width, width), 1, 2).reshape(27, width, full)]
where the time goes in v2:
time: 68.2 us; the launch traced here: 68 us
  Pallas kernels  57.9 us (85%)
  other arithmetic  7.38 us (11%)
  local copies, waits for them, and re-layouts  2.02 us (3%)
    pallas_call x1, Pallas kernels, body(): pl.pallas_call(functools.partial(kernel, n), out_shape=(jax.ShapeDtypeStr...  57.9 us
    convert_element_type x1, other arithmetic, body(): jnp.swapaxes(gw.reshape(27, 2, width, width), 1, 2).reshape(27, width, full)  3.72 us

profile of v2, /device:TPU:0, one launch (start us, length us, event | category | flops | bytes accessed | tf_op | source)
XLA Modules:
  0.0 68.0 jit_solution(12081529028890480705)
XLA Ops:
  0.6 0.9 %convert_reduce_fusion = f32[8]{0:T(128)S(1)} fusion(s32[8,27]{1,0:T(8,128)} %param.7), kind=kLoop, calls=%fused_computation.10 | loop fusion | flops 16 | bytes 64 | tf_op jit(solution)/shard_map/broadcast_in_dim | solution.py:357
  1.5 0.7 %fusion.4 = s32[2,8]{1,0:T(2,128)S(1)} fusion(s32[1,2,8]{2,1,0:T(2,128)} %param.8), kind=kLoop, calls=%fused_computation.13 | loop fusion | flops 48 | bytes 128 | tf_op jit(solution)/shard_map/jit(_where)/select_n | solution.py:358
  2.2 0.7 broadcast_in_dim.26.occ_ref
  2.8 0.7 %fusion.3 = s32[27,8]{0,1:T(8,128)S(1)} fusion(s32[8,27]{1,0:T(8,128)} %param.7), kind=kLoop, calls=%fused_computation.9 | loop fusion | flops 1728 | bytes 1728 | tf_op jit(solution)/shard_map/transpose | solution.py:356
  3.5 0.7 fusion.1.sel_ref
  4.2 0.1 copy.8
  4.3 0.7 %fusion.names_ref = f32[27,8,128]{2,1,0:T(8,128)} fusion(s32[27,8]{1,0:T(8,128)S(1)} %copy.8), kind=kLoop, calls=%fused_computation.3 | loop fusion | flops 55296 | bytes 111456 | tf_op jit(solution)/shard_map/convert_element_type | solution.py:356
  5.0 57.9 %shard_map.76 = (bf16[64,128]{1,0:T(8,128)(2,1)}, bf16[512,128]{1,0:T(8,128)(2,1)}, bf16[27,256,128]{2,1,0:T(8,128)(2,1)}) custom-call(bf16[512,128]{1,0:T(8,128)(2,1)} %bitcast.18, bf16[27,256,256]{2,1,0:T(8,128)(2,1)} %weight_ref.1, f32[27,8,128]{2,1,0:T(8,128)} %fusion.names_ref, f32[8,128]{1,0:T(8,128)} %broadcast_in_dim.26.occ_ref, ...), custom_call_target="tpu_custom_call" | custom-call | tf_op jit(solution)/shard_map/pallas_call | solution.py:365
  63.0 0.0 copy-start.1
  63.0 0.0 copy-start
  63.0 3.7 %copy_bitcast_fusion = f32[27,128,256]{2,1,0:T(8,128)} fusion(bf16[27,2,128,128]{3,2,1,0:T(8,128)(2,1)} %bitcast.16), kind=kLoop, calls=%fused_computation | loop fusion | flops 884736 | bytes 5308416 | tf_op jit(solution)/shard_map/convert_element_type | solution.py:410
  66.7 0.0 copy-done.1
  66.7 0.6 copy.14
  67.3 0.0 copy-done
  67.3 0.7 copy.15
Async XLA Ops:
  63.0 3.7 %copy-start.1 = (bf16[64,128]{1,0:T(8,128)(2,1)S(1)}, bf16[64,128]{1,0:T(8,128)(2,1)}, u32[]{:S(2)}) copy-start(bf16[64,128]{1,0:T(8,128)(2,1)} %get-tuple-element.6) | copy-start | bytes 49156
  63.0 4.3 %copy-start = (bf16[512,128]{1,0:T(8,128)(2,1)S(1)}, bf16[512,128]{1,0:T(8,128)(2,1)}, u32[]{:S(2)}) copy-start(bf16[512,128]{1,0:T(8,128)(2,1)} %get-tuple-element.7) | copy-start | bytes 393220

commit v3 on v2

--- a/solution.py
+++ b/solution.py
@@ -196,9 +196,9 @@
 
 
 def kernel(
-    n, feat_ref, weight_ref, names_ref, occ_ref, sel_ref, gp_ref,
+    n, feat_ref, weight_ref, near_ref, slots_ref, gp_ref,
     pooled_ref, gf_ref, gw_ref,
-    wf, wb, feat, flow, fhigh, grad, glow, ghigh, tile_in, tile_g, pick, merge,
+    wf, wb, feat, flow, fhigh, grad, glow, ghigh, tile_in, tile_g, pick, sel, merge,
     stage, pool_stage, wsem, fsend, frecv, gsend, grecv, ssend, srecv, total, rsem, *bufs,
 ):
     me, core = lax.axis_index("morton"), lax.axis_index("chan")
@@ -220,6 +220,26 @@
     others = [(sums[0].partner(bit)[1], core) for bit in sums[0].bits]
     for target in [(me, 1 - core), (nxt, 0), (nxt, 1), (prv, 0), (prv, 1)] + others:
         pl.semaphore_signal(barrier, inc=1, device_id=target, device_id_type=MESH)
+    lane = lax.broadcasted_iota(jnp.int32, (2 * blocks, width), 1)
+    row = lax.broadcasted_iota(jnp.int32, (2 * blocks, width), 0)
+    slots = slots_ref.shape[-1]
+    for side in range(2):
+        hit = row == lane - slots
+        for j in range(slots):
+            named = slots_ref[0, side, j]
+            hit = hit | ((lane == j) & (row == named + blocks) & (named < blocks))
+        sel[side] = jnp.where(hit, 1.0, 0.0).astype(F32)
+    near = near_ref[...]
+    mark = lane[:blocks]
+    for k in range(27):
+        name = jnp.broadcast_to(near[:, k : k + 1], (blocks, width))
+        if k // 9 != 1:
+            rim = jnp.where(name > blocks + slots, name - slots, name) - (blocks + 1)
+            name = jnp.where(name < blocks, name + slots, jnp.where(name == blocks, -1, rim))
+        else:
+            name = jnp.where(name < blocks, name, -1)
+        pick[k] = jnp.where(mark == name, 1.0, 0.0).astype(F32)
+    occ = jnp.where(jnp.broadcast_to(near[:, 13:14], (blocks, width)) < blocks, 1.0, 0.0)
     stage[...] = feat_ref[...].astype(F32)
     feat[core] = jnp.concatenate(
         [stage[pl.ds(p, blocks, stride=64), :] for p in range(64)], axis=0
@@ -227,34 +247,27 @@
     pl.semaphore_wait(barrier, 5 + len(others))
     sels = [
         pltpu.make_async_remote_copy(
-            src_ref=sel_ref.at[1], dst_ref=merge.at[0], send_sem=ssend.at[0],
+            src_ref=sel.at[1], dst_ref=merge.at[0], send_sem=ssend.at[0],
             recv_sem=srecv.at[0], device_id=(nxt, core), device_id_type=MESH,
         ),
         pltpu.make_async_remote_copy(
-            src_ref=sel_ref.at[0], dst_ref=merge.at[1], send_sem=ssend.at[1],
+            src_ref=sel.at[0], dst_ref=merge.at[1], send_sem=ssend.at[1],
             recv_sem=srecv.at[1], device_id=(prv, core), device_id_type=MESH,
         ),
     ]
     copies = rim_copies(feat, flow, fhigh, fsend, frecv, me, core, n)
     for copy in sels + copies:
         copy.start()
-    occ = occ_ref[...]
     fill_interior(tile_in, feat, occ, core, blocks)
     for copy in sels:
         copy.wait()
-    eye = (
-        lax.broadcasted_iota(jnp.int32, (blocks, width), 0)
-        == lax.broadcasted_iota(jnp.int32, (blocks, width), 1)
-    ).astype(F32)
-    pick[0:9] = jnp.dot(
-        names_ref[0:9].reshape(9 * blocks, width)[:, : 2 * blocks],
-        jnp.concatenate([eye, merge[0]], axis=0), preferred_element_type=F32,
-    ).reshape(9, blocks, width)
-    pick[9:18] = names_ref[9:18]
-    pick[18:27] = jnp.dot(
-        names_ref[18:27].reshape(9 * blocks, width)[:, : 2 * blocks],
-        jnp.concatenate([eye, merge[1]], axis=0), preferred_element_type=F32,
-    ).reshape(9, blocks, width)
+    for side in range(2):
+        ks = slice(18 * side, 18 * side + 9)
+        named = pick[ks].reshape(9 * blocks, width)
+        spread = lax.dot_general(
+            named, merge[side], (((1,), (1,)), ((), ())), preferred_element_type=F32
+        )
+        pick[ks, :, : 2 * blocks] = spread.reshape(9, blocks, 2 * blocks)
     wait_peer(feat, fsend, frecv, me, core)
     fill_interior(tile_in, feat, occ, 1 - core, blocks)
     wait_rims(feat, flow, fhigh, fsend, frecv, me, core)
@@ -348,15 +361,6 @@
     blocks = features.shape[0]
     width = features.shape[-1]
     full = weight.shape[-1]
-    slots = send_slots.shape[-1]
-    lanes = jnp.arange(width, dtype=jnp.int32)
-    column = jnp.where(neighbours > blocks, neighbours - 1, neighbours)
-    column = jnp.where(neighbours > blocks + slots, column - slots, column)
-    column = jnp.where(neighbours == blocks, -1, column)
-    names = (column.T[:, :, None] == lanes).astype(F32)
-    occ = jnp.broadcast_to((neighbours[:, 13] < blocks).astype(F32)[:, None], (blocks, width))
-    places = jnp.where(send_slots[0] < blocks, send_slots[0] + blocks, -1)
-    sel = (places[:, :, None] == lanes).astype(F32)
     rows = blocks * 64
     steps = len(bit_orders(n)[0])
     sizes = [max(full >> (step + 1), 16) for step in range(steps)]
@@ -369,7 +373,13 @@
             jax.ShapeDtypeStruct((rows, width), BF16),
             jax.ShapeDtypeStruct((27, full, width), BF16),
         ),
-        in_specs=[vmem, pl.BlockSpec(memory_space=pl.ANY), vmem, vmem, vmem, vmem],
+        in_specs=[
+            vmem,
+            pl.BlockSpec(memory_space=pl.ANY),
+            vmem,
+            pl.BlockSpec(memory_space=pltpu.SMEM),
+            vmem,
+        ],
         out_specs=(vmem, vmem, vmem),
         scratch_shapes=[
             pltpu.VMEM((27, full, width), BF16),
@@ -383,7 +393,8 @@
             pltpu.VMEM((2, 6, 6, 6, blocks, width), F32),
             pltpu.VMEM((2, 6, 6, 6, blocks, width), F32),
             pltpu.VMEM((27, blocks, width), F32),
-            pltpu.VMEM((2, slots, width), F32),
+            pltpu.VMEM((2, 2 * blocks, width), F32),
+            pltpu.VMEM((2, 2 * blocks, width), F32),
             pltpu.VMEM((rows, width), F32),
             pltpu.VMEM((2, blocks * 8, width), F32),
             pltpu.SemaphoreType.DMA((2,)),
@@ -401,7 +412,7 @@
             collective_id=0, has_side_effects=True, vmem_limit_bytes=60 * 1024 * 1024
         ),
     )(
-        features.reshape(rows, width), weight, names, occ, sel,
+        features.reshape(rows, width), weight, neighbours, send_slots,
         grad_pooled.reshape(blocks * 8, width),
     )
     return (

time: 68.2 us -> 64 us (0.938)
  other arithmetic: 7.38 us -> 3.72 us
  local copies, waits for them, and re-layouts: 2.02 us -> 1.27 us
    convert_element_type x2 -> x0, other arithmetic: 1.41 us -> none  [the longest x1 0.74 us: body(): names = (column.T[:, :, None] == lanes).astype(F32)]
    broadcast_in_dim x1 -> x0, other arithmetic: 0.87 us -> none  [body(): jnp.broadcast_to((neighbours[:, 13] < blocks).astype(F32)[:, None], (bloc...]
    transpose x1 -> x0, other arithmetic: 0.69 us -> none  [body(): names = (column.T[:, :, None] == lanes).astype(F32)]
    select_n x1 -> x0, other arithmetic: 0.68 us -> none  [body(): places = jnp.where(send_slots[0] < blocks, send_slots[0] + blocks, -1)]
where the time goes in v3:
time: 64 us; the launch traced here: 63.8 us
  Pallas kernels  58.2 us (91%)
  other arithmetic  3.72 us (6%)
  local copies, waits for them, and re-layouts  1.27 us (2%)
  between operations  0.66 us (1%)
    pallas_call x1, Pallas kernels, body(): pl.pallas_call(functools.partial(kernel, n), out_shape=(jax.ShapeDtypeStr...  58.2 us
    convert_element_type x1, other arithmetic, body(): jnp.swapaxes(gw.reshape(27, 2, width, width), 1, 2).reshape(27, width, full)  3.72 us

profile of v3, /device:TPU:0, one launch (start us, length us, event | category | flops | bytes accessed | tf_op | source)
XLA Modules:
  0.0 63.8 jit_solution(2802922487210181121)
XLA Ops:
  0.6 58.2 %shard_map.76 = (bf16[64,128]{1,0:T(8,128)(2,1)}, bf16[512,128]{1,0:T(8,128)(2,1)}, bf16[27,256,128]{2,1,0:T(8,128)(2,1)}) custom-call(bf16[512,128]{1,0:T(8,128)(2,1)} %bitcast.13, bf16[27,256,256]{2,1,0:T(8,128)(2,1)} %weight_ref.1, s32[8,27]{1,0:T(8,128)} %near_ref.1, s32[1,2,8]{2,1,0:T(2,128)} %slots_ref.1, bf16[64,128]{1,0:T(8,128)(2,1)} %bitcast.15), custom_call_target="tpu_custom_call" | custom-call | tf_op jit(solution)/shard_map/pallas_call | solution.py:369
  58.8 0.0 copy-start.1
  58.8 0.0 copy-start
  58.8 3.7 %copy_bitcast_fusion = f32[27,128,256]{2,1,0:T(8,128)} fusion(bf16[27,2,128,128]{3,2,1,0:T(8,128)(2,1)} %bitcast.12), kind=kLoop, calls=%fused_computation | loop fusion | flops 884736 | bytes 5308416 | tf_op jit(solution)/shard_map/convert_element_type | solution.py:421
  62.6 0.0 copy-done.1
  62.6 0.6 copy.13
  63.2 0.0 copy-done
  63.2 0.7 %copy.14 = bf16[8,4,4,4,128]{4,3,2,1,0:T(4,128)(2,1)} copy(bf16[8,4,4,4,128]{4,3,2,1,0:T(4,128)(2,1)S(1)} %bitcast.14) | data formatting | bytes 262144
Async XLA Ops:
  58.8 3.7 %copy-start.1 = (bf16[64,128]{1,0:T(8,128)(2,1)S(1)}, bf16[64,128]{1,0:T(8,128)(2,1)}, u32[]{:S(2)}) copy-start(bf16[64,128]{1,0:T(8,128)(2,1)} %get-tuple-element.6) | copy-start | bytes 49156
  58.8 4.3 %copy-start = (bf16[512,128]{1,0:T(8,128)(2,1)S(1)}, bf16[512,128]{1,0:T(8,128)(2,1)}, u32[]{:S(2)}) copy-start(bf16[512,128]{1,0:T(8,128)(2,1)} %get-tuple-element.7) | copy-start | bytes 393220
